TPU v7x, 32 devices: a whole 2x2x4 slice. The times are simulated.
32 devices in a mesh: row: 4 (over y, x), col: 8 (over z, core).
Axes of the slice: x: 2, y: 2, z: 4, core: 2. Of those that a mesh axis runs over, the one named last changes fastest.
Arguments:
- pair: bfloat16 [448, 448, 128], P('row', 'col'), may hold values from -6 to 6
- pair_mask: int32 [448, 448], P('row', 'col'), may hold values 0 or 1
- ln_in_gain: float32 [128], replicated, may hold values from 0.1 to 1.9
- proj_ab: bfloat16 [128, 512], replicated, may hold values from -0.5 to 0.5
- gate_weight: bfloat16 [128, 128], replicated, may hold values from -0.5 to 0.5
- ln_out_gain: float32 [128], replicated, may hold values from 0.1 to 1.9
- out_weight: bfloat16 [128, 128], replicated, may hold values from -0.5 to 0.5
Outputs:
- update: bfloat16 [448, 448, 128], P('row', 'col')
All inputs are finite; a program needn't handle non-finite values. No bound on the sum of `pair_mask` on one device may be relied on, other than what follows from the above.
Results may differ from a plain program's by a relative error of at most 0.008.
Values may be sent and summed in bfloat16 or wider, within the bound.
A program may use at most 192 MiB of HBM per device.

v0:
```python
import jax
import jax.numpy as jnp
from jax import lax
from jax.sharding import PartitionSpec as P

EPS = 1e-05


def broadcast(x, axis, root):
    mine = lax.axis_index(axis) == root
    return lax.psum(jnp.where(mine, x, jnp.zeros_like(x)), axis)


def layer_norm(values, gain):
    values = values.astype(jnp.float32)
    middle = jnp.mean(values, axis=-1, keepdims=True)
    centred = values - middle
    spread = jnp.mean(centred * centred, axis=-1, keepdims=True)
    return centred * lax.rsqrt(spread + EPS) * gain


def shards(pair, pair_mask, ln_in_gain, proj_ab, gate_weight, ln_out_gain, out_weight):
    rows_here, cols_here, channels = pair.shape
    hidden = out_weight.shape[0]
    normed = layer_norm(pair, ln_in_gain).astype(jnp.bfloat16).reshape(-1, channels)
    projected = jnp.dot(normed, proj_ab, preferred_element_type=jnp.float32)
    projected = projected.reshape(rows_here, cols_here, 4 * hidden)
    weight = pair_mask.astype(jnp.float32)[..., None]
    left = jax.nn.sigmoid(projected[..., 0:hidden]) * projected[..., hidden : 2 * hidden] * weight
    right = (
        jax.nn.sigmoid(projected[..., 2 * hidden : 3 * hidden])
        * projected[..., 3 * hidden : 4 * hidden]
        * weight
    )
    left = left.astype(jnp.bfloat16)
    right = right.astype(jnp.bfloat16)
    columns = lax.all_gather(left, "row", axis=0, tiled=True)
    ratio = lax.axis_size("col") // lax.axis_size("row")
    pieces = []
    for offset in range(ratio):
        source = lax.axis_index("row") * ratio + offset
        pieces.append(broadcast(columns, "col", source))
    left_panel = jnp.concatenate(pieces, axis=1)
    triangle = jnp.einsum(
        "kih,kjh->ijh",
        left_panel,
        lax.all_gather(right, "row", axis=0, tiled=True),
        preferred_element_type=jnp.float32,
    )
    tri_normed = layer_norm(triangle, ln_out_gain).astype(jnp.bfloat16).reshape(-1, hidden)
    gate = jax.nn.sigmoid(jnp.dot(normed, gate_weight, preferred_element_type=jnp.float32))
    mixed = jnp.dot(tri_normed, out_weight, preferred_element_type=jnp.float32)
    return (gate * mixed).astype(jnp.bfloat16).reshape(rows_here, cols_here, channels)


def solution(mesh):
    in_specs = (P("row", "col", None), P("row", "col"), P(), P(), P(), P(), P())
    out_specs = P("row", "col", None)
    return jax.shard_map(shards, mesh=mesh, in_specs=in_specs, out_specs=out_specs, check_vma=False)
```

profile of v0, /device:TPU:0, one launch (start us, length us, event | category | flops | bytes accessed | tf_op | source)
XLA Modules:
  0.0 770.9 jit_solution(9283072976378445667)
XLA Ops:
  6.5 0.0 copy-start
  6.5 0.0 all-gather.5.cloned.1.call-start
  6.6 2.4 convert_reduce_fusion
  9.0 0.1 copy.35
  9.1 0.1 copy.36
  9.2 3.0 fusion.10
  12.2 0.1 copy.37
  12.3 0.1 copy.38
  12.4 0.1 copy.39
  12.5 2.1 fusion.12
  14.7 1.8 fusion.23
  16.5 3.6 fusion.14
  20.1 0.0 all-gather.5.cloned.1.call-update
  20.1 0.0 all-gather.3.cloned.1.call-start
  20.1 0.7 all-gather.3.cloned.1.call-update
  20.8 0.2 all-reduce.3.cloned.1.call-start
  21.1 73.1 %all-gather.5.cloned.1.call-done = bf16[448,56,128]{2,1,0:T(8,128)(2,1)} async-done(((bf16[112,56,128]{2,1,0:T(8,128)(2,1)}), bf16[448,56,128]{2,1,0:T(8,128)(2,1)}) %all-gather.5.cloned.1.call-update) | async-done | bytes 6422544 | tf_op jit(solution)/shard_map/all_gather | solution.py:37
  94.2 20.9 %copy.40 = bf16[448,56,128]{1,0,2:T(8,128)(2,1)} copy(bf16[448,56,128]{2,1,0:T(8,128)(2,1)} %all-gather.5.cloned.1.call-done) | data formatting | bytes 12845056 | tf_op jit(solution)/shard_map/all_gather | solution.py:37
  115.1 16.6 %broadcast_select_fusion.1 = (bf16[448,56,128]{1,0,2:T(8,128)(2,1)}, bf16[448,56,128]{1,0,2:T(8,128)(2,1)}) fusion(bf16[448,56,128]{1,0,2:T(8,128)(2,1)} %copy.40, pred[]{:T(512)S(6)} %eq.6, pred[]{:T(512)S(6)} %eq.7), kind=kLoop, calls=%fused_computation.5 | loop fusion | flops 6422528 | bytes 19267586 | tf_op jit(solution)/shard_map/jit(_where)/select_n | solution.py:11
  131.7 0.0 all-reduce.3.cloned.1.call-update
  131.7 0.7 copy-done.7
  132.5 2.7 fusion.6
  135.2 32.2 %all-gather.3.cloned.1.call-done = bf16[448,56,128]{2,1,0:T(8,128)(2,1)} async-done(((bf16[112,56,128]{2,1,0:T(8,128)(2,1)}), bf16[448,56,128]{2,1,0:T(8,128)(2,1)}) %all-gather.3.cloned.1.call-update) | async-done | bytes 6422544 | tf_op jit(solution)/shard_map/all_gather | solution.py:47
  167.3 13.0 %copy.42 = bf16[448,56,128]{0,1,2:T(8,128)(2,1)} copy(bf16[448,56,128]{2,1,0:T(8,128)(2,1)} %all-gather.3.cloned.1.call-done) | data formatting | bytes 12845056 | tf_op jit(solution)/shard_map/all_gather | solution.py:47
  180.3 559.7 %all-reduce.3.cloned.1.call-done = (bf16[448,56,128]{1,0,2:T(8,128)(2,1)}, bf16[448,56,128]{1,0,2:T(8,128)(2,1)}) async-done(((bf16[448,56,128]{1,0,2:T(8,128)(2,1)}, bf16[448,56,128]{1,0,2:T(8,128)(2,1)}), (bf16[448,56,128]{1,0,2:T(8,128)(2,1)}, bf16[448,56,128]{1,0,2:T(8,128)(2,1)})) %all-reduce.3.cloned.1.call-update) | async-done | bytes 12845072 | tf_op jit(solution)/shard_map/psum | solution.py:11
  740.0 15.9 %bitcast_reduce_fusion = (f32[112,56]{0,1:T(8,128)S(1)}, f32[128,56,112]{2,1,0:T(8,128)S(1)}) fusion(bf16[448,56,128]{0,1,2:T(8,128)(2,1)} %copy.42, bf16[448,56,128]{1,0,2:T(8,128)(2,1)} %get-tuple-element.5, bf16[448,56,128]{1,0,2:T(8,128)(2,1)} %get-tuple-element.6), kind=kOutput, calls=%fused_computation.17 | convolution fusion | flops 745809792 | bytes 22503936 | tf_op jit(solution)/shard_map/kih,kjh->ijh/dot_general | solution.py:44
  755.9 0.0 copy-start.5
  755.9 0.5 multiply_reduce_fusion
  756.5 0.1 copy-done.5
  756.6 0.6 multiply_convert_fusion
  757.1 3.1 copy.43
  760.2 4.1 fusion.7
  (17 shorter events, 0.1 us)
Async XLA Ops:
  6.5 8.1 %copy-start = (bf16[128,512]{1,0:T(8,128)(2,1)S(1)}, bf16[128,512]{1,0:T(8,128)(2,1)}, u32[]{:S(2)}) copy-start(bf16[128,512]{1,0:T(8,128)(2,1)} %param.10) | copy-start | bytes 393220
  6.5 6.0 copy-start.2
  6.5 5.9 copy-start.4
  6.5 6.0 copy-start.6
  6.5 87.6 %all-gather.5.cloned.1.call-start = ((), (), s32[]{:S(2)}) async-start(), calls=%async_computation.1 | async-start | bytes 8028160 | tf_op jit(solution)/shard_map/all_gather | solution.py:37
  20.1 147.2 %all-gather.3.cloned.1.call-start = ((), (), s32[]{:S(2)}) async-start(), calls=%async_computation | async-start | bytes 8028160 | tf_op jit(solution)/shard_map/all_gather | solution.py:47
  20.8 719.2 %all-reduce.3.cloned.1.call-start = ((), (), s32[]{:S(2)}) async-start(), calls=%async_computation.2 | async-start | bytes 58720256 | tf_op jit(solution)/shard_map/psum | solution.py:11
  131.7 0.8 copy-start.7
  755.9 0.7 copy-start.5
  756.6 3.7 copy-start.3
  760.2 4.2 copy-start.1
Sparse Core Ops, SparseCore 0:
  20.2 73.9 all-gather.4
  96.0 71.2 all-gather.2
  169.9 570.0 all-reduce.2
where the time goes:
time: 772 us; the launch traced here: 771 us
  waiting for transfers between devices  666 us (86%)
  local copies, waits for them, and re-layouts  38.2 us (5%)
  other arithmetic  28.9 us (4%)
  matrix products  24.5 us (3%)
  between operations  13.3 us (2%)
    psum x1, waiting for transfers between devices, broadcast(): return lax.psum(jnp.where(mine, x, jnp.zeros_like(x)), axis)  560 us
    all_gather x1, waiting for transfers between devices, shards(): columns = lax.all_gather(left, 'row', axis=0, tiled=True)  73.1 us
    all_gather x1, waiting for transfers between devices, shards(): lax.all_gather(right, 'row', axis=0, tiled=True)  32.2 us
    all_gather x1, local copies, waits for them, and re-layouts, shards(): columns = lax.all_gather(left, 'row', axis=0, tiled=True)  20.9 us
    select_n x1, other arithmetic, broadcast(): return lax.psum(jnp.where(mine, x, jnp.zeros_like(x)), axis)  16.6 us
    dot_general x1, matrix products, shards(): jnp.einsum('kih,kjh->ijh', left_panel, lax.all_gather(right, 'row', axis=...  15.9 us
  transfers between devices with their start and end apart: 3, of which 3 were waited for; matrix products, arithmetic and copies ran while one was open for 7% of the time, Pallas kernels for 0%

commit v1 on v0

v1 whole, which is shorter than its diff:
```python
import jax
import jax.numpy as jnp
from jax import lax
from jax.sharding import PartitionSpec as P

EPS = 1e-05
AXES = ("row", "col")


def layer_norm(values, gain, axis):
    values = values.astype(jnp.float32)
    middle = jnp.mean(values, axis=axis, keepdims=True)
    centred = values - middle
    spread = jnp.mean(centred * centred, axis=axis, keepdims=True)
    return centred * lax.rsqrt(spread + EPS) * gain


def shards(pair, pair_mask, ln_in_gain, proj_ab, gate_weight, ln_out_gain, out_weight):
    rows_here, cols_here, channels = pair.shape
    hidden = out_weight.shape[0]
    tokens = rows_here * cols_here
    n_row, n_col = lax.axis_size("row"), lax.axis_size("col")
    devices = n_row * n_col
    part = hidden // devices
    ratio = n_col // n_row
    normed = layer_norm(pair, ln_in_gain, -1).astype(jnp.bfloat16).reshape(tokens, channels)
    projected = jnp.einsum("tc,ch->ht", normed, proj_ab, preferred_element_type=jnp.float32)
    weight = pair_mask.astype(jnp.float32).reshape(1, tokens)
    left = jax.nn.sigmoid(projected[0:hidden]) * projected[hidden : 2 * hidden] * weight
    right = jax.nn.sigmoid(projected[2 * hidden : 3 * hidden]) * projected[3 * hidden :] * weight
    both = jnp.stack([left.reshape(devices, part, tokens), right.reshape(devices, part, tokens)], axis=1)
    both = both.astype(jnp.bfloat16).reshape(devices, 2 * part, tokens)
    both = lax.all_to_all(both, AXES, 0, 0)
    both = both.reshape(n_row, n_col, 2, part, rows_here, cols_here)
    both = both.transpose(2, 3, 0, 4, 1, 5).reshape(2, part, n_row * rows_here, n_col * cols_here)
    triangle = jnp.einsum("hki,hkj->hij", both[0], both[1], preferred_element_type=jnp.float32)
    triangle = triangle.astype(jnp.bfloat16).reshape(part, n_row, rows_here, n_col, cols_here)
    triangle = triangle.transpose(1, 3, 0, 2, 4).reshape(devices, part, tokens)
    triangle = lax.all_to_all(triangle, AXES, 0, 0).reshape(hidden, tokens)
    tri_normed = layer_norm(triangle, ln_out_gain[:, None], 0).astype(jnp.bfloat16)
    gate = jax.nn.sigmoid(jnp.dot(normed, gate_weight, preferred_element_type=jnp.float32))
    mixed = jnp.einsum("ht,hc->tc", tri_normed, out_weight, preferred_element_type=jnp.float32)
    return (gate * mixed).astype(jnp.bfloat16).reshape(rows_here, cols_here, channels)


def solution(mesh):
    in_specs = (P("row", "col", None), P("row", "col"), P(), P(), P(), P(), P())
    out_specs = P("row", "col", None)
    return jax.shard_map(shards, mesh=mesh, in_specs=in_specs, out_specs=out_specs, check_vma=False)
```

time: 772 us -> 214 us (0.28)
  waiting for transfers between devices: 666 us -> 36.7 us
  blocking collectives: 0 us -> 81.3 us
  local copies, waits for them, and re-layouts: 38.2 us -> 66.9 us
  other arithmetic: 28.9 us -> 11.4 us
  between operations: 13.3 us -> 0.24 us
  matrix products: 24.5 us -> 13.3 us
    psum x1 -> x0, waiting for transfers between devices: 560 us -> none  [broadcast(): return lax.psum(jnp.where(mine, x, jnp.zeros_like(x)), axis)]
    all_gather x2 -> x0, waiting for transfers between devices: 105 us -> none  [the longest x1 73.1 us: shards(): columns = lax.all_gather(left, 'row', axis=0, tiled=True)]
    all_to_all x0 -> x1, blocking collectives: none -> 81.3 us  [shards(): both = lax.all_to_all(both, AXES, 0, 0)]
    all_to_all x0 -> x1, waiting for transfers between devices: none -> 36.7 us  [shards(): triangle = lax.all_to_all(triangle, AXES, 0, 0).reshape(hidden, tokens)]
    all_gather x2 -> x0, local copies, waits for them, and re-layouts: 33.9 us -> none  [the longest x1 20.9 us: shards(): columns = lax.all_gather(left, 'row', axis=0, tiled=True)]
    reshape x0 -> x4, local copies, waits for them, and re-layouts: none -> 28.9 us  [the longest x2 13.8 us: shards(): triangle = triangle.transpose(1, 3, 0, 2, 4).reshape(devices, part, tokens)]
    slice x0 -> x3, local copies, waits for them, and re-layouts: none -> 19 us  [the longest x2 13.2 us: shards(): both[1]]
    select_n x1 -> x0, other arithmetic: 16.6 us -> none  [broadcast(): return lax.psum(jnp.where(mine, x, jnp.zeros_like(x)), axis)]
  transfers between devices with their start and end apart: 3 -> 1, of which waited for: 3 -> 1; matrix products, arithmetic and copies ran while one was open for 7% -> 1% of each run, Pallas kernels for 0% -> 0%
where the time goes in v1:
time: 214 us; the launch traced here: 213 us
  blocking collectives  81.3 us (38%)
  local copies, waits for them, and re-layouts  66.9 us (31%)
  waiting for transfers between devices  36.7 us (17%)
  matrix products  13.3 us (6%)
  other arithmetic  11.4 us (5%)
  starting transfers between devices  2.91 us (1%)
    all_to_all x1, blocking collectives, shards(): both = lax.all_to_all(both, AXES, 0, 0)  81.3 us
    all_to_all x1, waiting for transfers between devices, shards(): triangle = lax.all_to_all(triangle, AXES, 0, 0).reshape(hidden, tokens)  36.7 us
    reshape x2, local copies, waits for them, and re-layouts, shards(): triangle = triangle.transpose(1, 3, 0, 2, 4).reshape(devices, part, tokens)  13.8 us
    slice x2, local copies, waits for them, and re-layouts, shards(): both[1]  13.2 us
    reshape x1, local copies, waits for them, and re-layouts, shards(): both = both.reshape(n_row, n_col, 2, part, rows_here, cols_here)  13.1 us
    another operation x4, local copies, waits for them, and re-layouts, shards(): jnp.stack([left.reshape(devices, part, tokens), right.reshape(devices, pa...  5.91 us
    slice x1, local copies, waits for them, and re-layouts, shards(): both[0]  5.72 us
    dot_general x1, matrix products, shards(): jnp.einsum('ht,hc->tc', tri_normed, out_weight, preferred_element_type=jn...  4.86 us
  transfers between devices with their start and end apart: 1, of which 1 were waited for; matrix products, arithmetic and copies ran while one was open for 1% of the time, Pallas kernels for 0%

profile of v1, /device:TPU:0, one launch (start us, length us, event | category | flops | bytes accessed | tf_op | source)
XLA Modules:
  0.0 212.7 jit_solution(8897927441303021284)
XLA Ops:
  0.0 2.5 %convert_reduce_fusion = f32[112,56]{1,0:T(8,128)S(1)} fusion(bf16[112,56,128]{2,1,0:T(8,128)(2,1)} %param.7), kind=kLoop, calls=%fused_computation.8 | loop fusion | flops 1599360 | bytes 1630720 | tf_op jit(solution)/shard_map/reduce_sum | solution.py:12
  2.5 3.0 %fusion.6 = f32[112,56]{1,0:T(8,128)S(1)} fusion(bf16[112,56,128]{2,1,0:T(8,128)(2,1)} %param.7, f32[112,56]{1,0:T(8,128)S(1)} %broadcast_multiply_fusion), kind=kLoop, calls=%fused_computation.11 | loop fusion | flops 3204992 | bytes 1655808 | tf_op jit(solution)/shard_map/reduce_sum | solution.py:14
  5.5 0.1 copy.28
  5.6 0.1 mul.70
  5.8 2.1 fusion.8
  7.9 1.9 convolution_bitcast_fusion
  9.8 1.7 fusion.15
  11.5 1.4 stack_reshape.8
  12.9 1.6 copy.29
  14.5 1.4 stack_reshape.9
  15.9 1.6 copy.30
  17.4 0.3 pad_maximum_fusion
  17.8 0.9 copy.31
  18.7 81.3 %all_to_all.10 = bf16[32,8,6272]{2,1,0:T(8,128)(2,1)S(1)} all-to-all(bf16[32,8,6272]{2,1,0:T(8,128)(2,1)S(1)} %copy.31), channel_id=1, replica_groups=mesh['row'=4,'col'=8] {'row','col'}, dimensions={0} | all-to-all | bytes 6422528 | tf_op jit(solution)/shard_map/all_to_all | solution.py:33
  100.0 13.1 %reshape.60 = bf16[4,8,2,4,112,56]{5,4,3,2,1,0:T(8,128)(2,1)} reshape(bf16[32,8,6272]{2,1,0:T(8,128)(2,1)S(1)} %all_to_all.10) | data formatting | bytes 6422528 | tf_op jit(solution)/shard_map/reshape | solution.py:34
  113.1 7.5 %fusion.22 = (bf16[1,4,4,112,8,56]{5,3,1,0,4,2:T(8,128)(2,1)}, bf16[1,4,4,112,8,56]{5,3,1,0,4,2:T(8,128)(2,1)}) fusion(bf16[2,4,4,112,8,56]{5,3,1,0,4,2:T(8,128)(2,1)} %bitcast.22), kind=kLoop, calls=%fused_computation.40 | loop fusion | bytes 6422528 | tf_op jit(solution)/shard_map/slice | solution.py:36
  120.6 5.7 %copy.33 = bf16[1,4,4,112,8,56]{3,2,5,4,1,0:T(4,128)(2,1)} copy(bf16[1,4,4,112,8,56]{5,3,1,0,4,2:T(8,128)(2,1)} %get-tuple-element.7) | data formatting | bytes 3211264 | tf_op jit(solution)/shard_map/slice | solution.py:36
  126.3 3.2 %reshape.66 = bf16[4,448,448]{1,2,0:T(8,128)(2,1)S(1)} reshape(bf16[1,4,4,112,8,56]{3,2,5,4,1,0:T(4,128)(2,1)} %copy.33) | data formatting | bytes 3211264 | tf_op jit(solution)/shard_map/squeeze | solution.py:36
  129.5 5.7 %copy.32 = bf16[1,4,4,112,8,56]{3,2,5,4,1,0:T(4,128)(2,1)} copy(bf16[1,4,4,112,8,56]{5,3,1,0,4,2:T(8,128)(2,1)} %get-tuple-element.8) | data formatting | bytes 3211264 | tf_op jit(solution)/shard_map/slice | solution.py:36
  135.2 4.2 %squeeze.6 = bf16[4,448,448]{1,2,0:T(8,128)(2,1)} reshape(bf16[1,4,4,112,8,56]{3,2,5,4,1,0:T(4,128)(2,1)} %copy.32) | data formatting | bytes 3211264 | tf_op jit(solution)/shard_map/squeeze | solution.py:36
  139.5 3.9 %convolution_convert_fusion = bf16[4,448,448]{2,1,0:T(8,128)(2,1)} fusion(bf16[4,448,448]{1,2,0:T(8,128)(2,1)} %squeeze.6, bf16[4,448,448]{1,2,0:T(8,128)(2,1)S(1)} %reshape.66), kind=kOutput, calls=%fused_computation.31 | convolution fusion | flops 720125952 | bytes 4816896 | tf_op jit(solution)/shard_map/hki,hkj->hij/dot_general | solution.py:36
  143.4 2.7 %copy.35 = bf16[4,448,448]{1,2,0:T(8,128)(2,1)S(1)} copy(bf16[4,448,448]{2,1,0:T(8,128)(2,1)} %convolution_convert_fusion) | data formatting | bytes 3211264 | tf_op jit(solution)/shard_map/convert_element_type | solution.py:37
  146.0 2.1 reshape.61
  148.1 5.8 %copy.40 = bf16[4,8,4,112,56]{4,3,2,1,0:T(8,128)(2,1)} copy(bf16[4,8,4,112,56]{3,0,4,1,2:T(4,128)(2,1)} %bitcast.26) | data formatting | bytes 3211264 | tf_op jit(solution)/shard_map/reshape | solution.py:38
  153.9 8.0 %reshape.67 = bf16[32,4,6272]{2,1,0:T(4,128)(2,1)} reshape(bf16[4,8,4,112,56]{4,3,2,1,0:T(8,128)(2,1)} %copy.40) | data formatting | bytes 3211264 | tf_op jit(solution)/shard_map/reshape | solution.py:38
  161.9 2.9 %all-to-all-start.1 = ((bf16[32,4,6272]{2,1,0:T(4,128)(2,1)}), bf16[32,4,6272]{2,1,0:T(4,128)(2,1)S(1)}, u32[]{:S(2)}, u32[]{:S(2)}) async-start(bf16[32,4,6272]{2,1,0:T(4,128)(2,1)} %reshape.67), calls=%async_computation.1 | async-start | bytes 3211264 | tf_op jit(solution)/shard_map/all_to_all | solution.py:39
  164.9 2.7 %fusion.2 = f32[6272,128]{1,0:T(8,128)} fusion(bf16[6272,128]{1,0:T(8,128)(2,1)S(1)} %bitcast.25, bf16[128,128]{1,0:T(8,128)(2,1)S(1)} %copy-done.9), kind=kOutput, calls=%fused_computation.5 | convolution fusion | flops 207929344 | bytes 4849664 | tf_op jit(solution)/shard_map/dot_general | solution.py:41
  167.5 36.7 %all-to-all-done.1 = bf16[32,4,6272]{2,1,0:T(4,128)(2,1)S(1)} async-done(((bf16[32,4,6272]{2,1,0:T(4,128)(2,1)}), bf16[32,4,6272]{2,1,0:T(4,128)(2,1)S(1)}, u32[]{:S(2)}, u32[]{:S(2)}) %all-to-all-start.1) | async-done | bytes 1605664 | tf_op jit(solution)/shard_map/all_to_all | solution.py:39
  204.2 0.7 convert_reduce_fusion.1
  204.9 1.1 multiply_reduce_fusion
  206.0 1.8 reshape.64
  207.8 4.9 %fusion.3 = bf16[6272,128]{1,0:T(8,128)(2,1)} fusion(f32[6272,128]{1,0:T(8,128)} %fusion.2, bf16[128,128]{1,0:T(8,128)(2,1)S(1)} %copy-done.5, f32[128,6272]{1,0:T(8,128)} %reshape.64, f32[128]{0:T(128)S(1)} %copy-done.7, f32[6272]{0:T(1024)S(1)} %add_rsqrt_fusion.1, f32[6272]{0:T(1024)S(1)} %broadcast_multiply_fusion.1), kind=kOutput, calls=%fused_computation.6 | convolution fusion | flops 210337792 | bytes 8111616 | tf_op jit(solution)/shard_map/ht,hc->tc/dot_general | solution.py:42
  (25 shorter events, 0.1 us)
Async XLA Ops:
  0.0 7.9 %copy-start = (bf16[128,512]{1,0:T(8,128)(2,1)S(1)}, bf16[128,512]{1,0:T(8,128)(2,1)}, u32[]{:S(2)}) copy-start(bf16[128,512]{1,0:T(8,128)(2,1)} %param.10) | copy-start | bytes 393220
  0.0 5.7 %copy-start.2 = (bf16[112,56,128]{2,1,0:T(8,128)(2,1)S(1)}, bf16[112,56,128]{2,1,0:T(8,128)(2,1)}, u32[]{:S(2)}) copy-start(bf16[112,56,128]{2,1,0:T(8,128)(2,1)} %param.7) | copy-start | bytes 4816900
  0.0 5.5 %copy-start.6 = (s32[112,56]{0,1:T(8,128)S(1)}, s32[112,56]{0,1:T(8,128)}, u32[]{:S(2)}) copy-start(s32[112,56]{0,1:T(8,128)} %param.8) | copy-start | bytes 75268
  0.0 5.7 %copy-start.8 = (f32[128]{0:T(128)S(1)}, f32[128]{0:T(128)}, u32[]{:S(2)}) copy-start(f32[128]{0:T(128)} %param.9) | copy-start | bytes 1540
  7.9 1.9 copy-start.3
  153.9 11.0 %copy-start.4 = (bf16[112,56,128]{2,1,0:T(8,128)(2,1)S(1)}, bf16[112,56,128]{2,1,0:T(8,128)(2,1)}, u32[]{:S(2)}) copy-start(bf16[112,56,128]{2,1,0:T(8,128)(2,1)} %copy-done.3) | copy-start | bytes 4816900
  153.9 11.0 %copy-start.9 = (bf16[128,128]{1,0:T(8,128)(2,1)S(1)}, bf16[128,128]{1,0:T(8,128)(2,1)}, u32[]{:S(2)}) copy-start(bf16[128,128]{1,0:T(8,128)(2,1)} %param.11) | copy-start | bytes 98308
  161.9 42.3 %all-to-all-start.1 = ((bf16[32,4,6272]{2,1,0:T(4,128)(2,1)}), bf16[32,4,6272]{2,1,0:T(4,128)(2,1)S(1)}, u32[]{:S(2)}, u32[]{:S(2)}) async-start(bf16[32,4,6272]{2,1,0:T(4,128)(2,1)} %reshape.67), calls=%async_computation.1 | async-start | bytes 3211264 | tf_op jit(solution)/shard_map/all_to_all | solution.py:39
  204.9 3.0 %copy-start.5 = (bf16[128,128]{1,0:T(8,128)(2,1)S(1)}, bf16[128,128]{1,0:T(8,128)(2,1)}, u32[]{:S(2)}) copy-start(bf16[128,128]{1,0:T(8,128)(2,1)} %param.13) | copy-start | bytes 98308
  204.9 3.0 %copy-start.7 = (f32[128]{0:T(128)S(1)}, f32[128]{0:T(128)}, u32[]{:S(2)}) copy-start(f32[128]{0:T(128)} %param.12) | copy-start | bytes 1540
  206.0 6.7 %copy-start.1 = (bf16[128,512]{1,0:T(8,128)(2,1)S(1)}, bf16[128,512]{1,0:T(8,128)(2,1)}, u32[]{:S(2)}) copy-start(bf16[128,512]{1,0:T(8,128)(2,1)} %param.10) | copy-start | bytes 393220

commit v2 on v1

v2 whole, which is shorter than its diff:
```python
import functools

import jax
import jax.numpy as jnp
from jax import lax
from jax.experimental import pallas as pl
from jax.experimental.pallas import tpu as pltpu
from jax.sharding import PartitionSpec as P

EPS = 1e-05
LANES = 128
VMEM_LIMIT = 56 * 1024 * 1024
VMEM = pl.BlockSpec(memory_space=pltpu.VMEM)
ANY = pl.BlockSpec(memory_space=pl.ANY)


def chunks(length, size):
    return [(at, min(at + size, length)) for at in range(0, length, size)]


def pad_rows(values, to):
    short = to - values.shape[-2]
    if short == 0:
        return values
    shape = values.shape[:-2] + (short, values.shape[-1])
    return jnp.concatenate([values, jnp.zeros(shape, values.dtype)], axis=-2)


def layer_norm(values, gain, axis):
    middle = jnp.mean(values, axis=axis, keepdims=True)
    centred = values - middle
    spread = jnp.mean(centred * centred, axis=axis, keepdims=True)
    return centred * lax.rsqrt(spread + EPS) * gain


def operands_kernel(pair_ref, mask_ref, gain_ref, gates_ref, values_ref, normed_ref, out_ref):
    cols, padded = out_ref.shape[1], out_ref.shape[2]
    for low, high in chunks(cols, 8):
        normed = layer_norm(pair_ref[:, low:high, :].astype(jnp.float32), gain_ref[...], -1)
        normed_ref[:, low:high, :] = normed.astype(jnp.bfloat16)
        turned = pad_rows(jnp.transpose(normed, (1, 0, 2)), padded).astype(jnp.bfloat16)
        mine = []
        for at in range(high - low):
            turn = (((1,), (1,)), ((), ()))
            gates = lax.dot_general(gates_ref[...], turned[at], turn, preferred_element_type=jnp.float32)
            values = lax.dot_general(values_ref[...], turned[at], turn, preferred_element_type=jnp.float32)
            mine.append(jax.nn.sigmoid(gates) * values * mask_ref[low + at : low + at + 1, :])
        out_ref[:, low:high, :] = jnp.transpose(jnp.stack(mine), (1, 0, 2)).astype(jnp.bfloat16)


def exchange_kernel(
    n_row, n_col, rows, send_ref, out_ref, held, product, send_sem, recv_sem, back_sem, land_sem, own_sem
):
    part, _, _, cols, padded = held.shape
    devices = n_row * n_col
    row, col = lax.axis_index("row"), lax.axis_index("col")
    me = row * n_col + col

    def place(offset):
        other = lax.rem(me + offset, devices)
        return other, (other // n_col, lax.rem(other, n_col))

    barrier = pltpu.get_barrier_semaphore()

    def greet(offset, carry):
        pl.semaphore_signal(barrier, inc=1, device_id=place(offset)[1], device_id_type=pl.DeviceIdType.MESH)
        return carry

    lax.fori_loop(1, devices, greet, 0)
    pl.semaphore_wait(barrier, devices - 1)

    def scatter(h):
        pltpu.make_async_copy(send_ref.at[h, me], held.at[h, me], own_sem.at[h]).start()

        def one(offset, carry):
            other, device = place(offset)
            pltpu.make_async_remote_copy(
                src_ref=send_ref.at[h, other],
                dst_ref=held.at[h, me],
                send_sem=send_sem.at[h],
                recv_sem=recv_sem.at[h],
                device_id=device,
                device_id_type=pl.DeviceIdType.MESH,
            ).start()
            return carry

        lax.fori_loop(1, devices, one, 0)

    for h in range(part):
        scatter(h)

    def wait_others(ref, sem):
        some = ref.at[pl.ds(0, devices - 1)]
        pltpu.make_async_copy(some, some, sem).wait()

    def channel(h, carry):
        wait_others(held.at[h], recv_sem.at[h])
        pltpu.make_async_copy(send_ref.at[h, me], held.at[h, me], own_sem.at[h]).wait()
        sides = []
        for side in range(2):
            pieces = [
                held[h, at * n_col : (at + 1) * n_col, side].reshape(n_col * cols, padded) for at in range(n_row)
            ]
            sides.append(jnp.concatenate(pieces, axis=1))
        left, right = sides
        for at in range(n_row):
            panel = pad_rows(left[at * rows : (at + 1) * rows], padded)
            tri = lax.dot_general(right, panel, (((1,), (1,)), ((), ())), preferred_element_type=jnp.float32)
            product[h, at * n_col : (at + 1) * n_col] = tri.reshape(n_col, cols, padded).astype(jnp.bfloat16)
        pltpu.make_async_copy(product.at[h, me], out_ref.at[h, me], own_sem.at[h]).start()

        def one(offset, inner):
            other, device = place(offset)
            pltpu.make_async_remote_copy(
                src_ref=product.at[h, other],
                dst_ref=out_ref.at[h, me],
                send_sem=back_sem.at[h],
                recv_sem=land_sem.at[h],
                device_id=device,
                device_id_type=pl.DeviceIdType.MESH,
            ).start()
            return inner

        lax.fori_loop(1, devices, one, 0)
        return carry

    lax.fori_loop(0, part, channel, 0)

    def finish(h, carry):
        wait_others(out_ref.at[h], land_sem.at[h])
        pltpu.make_async_copy(product.at[h, me], out_ref.at[h, me], own_sem.at[h]).wait()
        wait_others(held.at[h], send_sem.at[h])
        wait_others(product.at[h], back_sem.at[h])
        return carry

    lax.fori_loop(0, part, finish, 0)


def update_kernel(tri_ref, normed_ref, gain_ref, gate_ref, weight_ref, out_ref):
    rows, cols, channels = normed_ref.shape
    for low, high in chunks(cols, 8):
        tri = layer_norm(tri_ref[:, low:high, :].astype(jnp.float32), gain_ref[...], 0)
        tri = jnp.transpose(tri, (1, 0, 2)).astype(jnp.bfloat16)
        mixed = []
        for at in range(high - low):
            turn = (((0,), (0,)), ((), ()))
            mixed.append(lax.dot_general(tri[at], weight_ref[...], turn, preferred_element_type=jnp.float32)[:rows])
        mixed = jnp.transpose(jnp.stack(mixed), (1, 0, 2))
        normed = normed_ref[:, low:high, :].astype(jnp.float32).reshape(rows * (high - low), channels)
        gate = jnp.dot(normed.astype(jnp.bfloat16), gate_ref[...], preferred_element_type=jnp.float32)
        gate = jax.nn.sigmoid(gate).reshape(rows, high - low, channels)
        out_ref[:, low:high, :] = (gate * mixed).astype(jnp.bfloat16)


def shards(pair, pair_mask, ln_in_gain, proj_ab, gate_weight, ln_out_gain, out_weight):
    rows, cols, channels = pair.shape
    hidden = out_weight.shape[0]
    n_row, n_col = lax.axis_size("row"), lax.axis_size("col")
    devices = n_row * n_col
    part = hidden // devices
    padded = -(-rows // LANES) * LANES
    plain = pltpu.CompilerParams(vmem_limit_bytes=VMEM_LIMIT)
    columns = proj_ab.reshape(channels, 2, 2, devices, part).transpose(2, 4, 3, 1, 0).reshape(2, 2 * hidden, channels)
    weight = jnp.pad(pair_mask.astype(jnp.float32).T, ((0, 0), (0, padded - rows)))
    normed, operands = pl.pallas_call(
        operands_kernel,
        out_shape=(
            jax.ShapeDtypeStruct((rows, cols, channels), jnp.bfloat16),
            jax.ShapeDtypeStruct((2 * hidden, cols, padded), jnp.bfloat16),
        ),
        in_specs=[VMEM] * 5,
        out_specs=(VMEM, VMEM),
        compiler_params=plain,
        name="operands",
    )(pair, weight, ln_in_gain.reshape(1, 1, channels), columns[0], columns[1])
    tri = pl.pallas_call(
        functools.partial(exchange_kernel, n_row, n_col, rows),
        out_shape=jax.ShapeDtypeStruct((part, devices, cols, padded), jnp.bfloat16),
        in_specs=[ANY],
        out_specs=ANY,
        scratch_shapes=[
            pltpu.VMEM((part, devices, 2, cols, padded), jnp.bfloat16),
            pltpu.VMEM((part, devices, cols, padded), jnp.bfloat16),
        ]
        + [pltpu.SemaphoreType.DMA((part,))] * 5,
        compiler_params=pltpu.CompilerParams(collective_id=0, has_side_effects=True, vmem_limit_bytes=VMEM_LIMIT),
        name="exchange",
    )(operands.reshape(part, devices, 2, cols, padded))
    gain = ln_out_gain.reshape(devices, part).T.reshape(hidden, 1, 1)
    mixing = out_weight.reshape(devices, part, channels).transpose(1, 0, 2).reshape(hidden, channels)
    return pl.pallas_call(
        update_kernel,
        out_shape=jax.ShapeDtypeStruct((rows, cols, channels), jnp.bfloat16),
        in_specs=[VMEM] * 5,
        out_specs=VMEM,
        compiler_params=plain,
        name="update",
    )(tri.reshape(hidden, cols, padded), normed, gain, gate_weight, mixing)


def solution(mesh):
    in_specs = (P("row", "col", None), P("row", "col"), P(), P(), P(), P(), P())
    out_specs = P("row", "col", None)
    return jax.shard_map(shards, mesh=mesh, in_specs=in_specs, out_specs=out_specs, check_vma=False)
```

time: 214 us -> 148 us (0.69)
  Pallas kernels: 0 us -> 142 us
  blocking collectives: 81.3 us -> 0 us
  local copies, waits for them, and re-layouts: 66.9 us -> 4.61 us
  waiting for transfers between devices: 36.7 us -> 0 us
  matrix products: 13.3 us -> 0 us
  other arithmetic: 11.4 us -> 0.75 us
  starting transfers between devices: 2.91 us -> 0 us
    pallas_call x0 -> x3, Pallas kernels: none -> 142 us  [the longest x1 126 us: shards(): pl.pallas_call(functools.partial(exchange_kernel, n_row, n_col, rows), ou...]
    all_to_all x1 -> x0, blocking collectives: 81.3 us -> none  [shards(): both = lax.all_to_all(both, AXES, 0, 0)]
    all_to_all x1 -> x0, waiting for transfers between devices: 36.7 us -> none  [shards(): triangle = lax.all_to_all(triangle, AXES, 0, 0).reshape(hidden, tokens)]
    reshape x4 -> x3, local copies, waits for them, and re-layouts: 28.9 us -> 1.48 us  [the longest x2 0.87 us: shards(): gain = ln_out_gain.reshape(devices, part).T.reshape(hidden, 1, 1)]
    slice x3, local copies, waits for them, and re-layouts: 19 us -> 1.42 us  [the longest x2 0.72 us: shards(): columns[1]]
    dot_general x4 -> x0, matrix products: 13.3 us -> none  [the longest x1 4.86 us: shards(): jnp.einsum('ht,hc->tc', tri_normed, out_weight, preferred_element_type=jn...]
    squeeze x2 -> x0, local copies, waits for them, and re-layouts: 7.45 us -> none  [the longest x1 4.23 us: shards(): both[0]]
    reduce_sum x4 -> x0, other arithmetic: 7.19 us -> none  [the longest x2 4.07 us: layer_norm(): spread = jnp.mean(centred * centred, axis=axis, keepdims=True)]
  transfers between devices with their start and end apart: 1 -> 0, of which waited for: 1 -> 0; matrix products, arithmetic and copies ran while one was open for 1% -> 0% of each run, Pallas kernels for 0% -> 0%
where the time goes in v2:
time: 148 us; the launch traced here: 147 us
  Pallas kernels  142 us (96%)
  local copies, waits for them, and re-layouts  4.61 us (3%)
    pallas_call x1, Pallas kernels, shards(): pl.pallas_call(functools.partial(exchange_kernel, n_row, n_col, rows), ou...  126 us
    pallas_call x1, Pallas kernels, shards(): pl.pallas_call(operands_kernel, out_shape=(jax.ShapeDtypeStruct((rows, co...  8.54 us
    pallas_call x1, Pallas kernels, shards(): pl.pallas_call(update_kernel, out_shape=jax.ShapeDtypeStruct((rows, cols,...  7.14 us

profile of v2, /device:TPU:0, one launch (start us, length us, event | category | flops | bytes accessed | tf_op | source)
XLA Modules:
  0.0 147.4 jit_solution(4352063596152314846)
XLA Ops:
  0.0 1.0 copy.12
  1.1 0.7 copy.13
  1.8 0.7 copy.14
  2.5 0.8 convert_bitcast_fusion
  3.2 0.6 pad.4.mask_ref
  3.8 8.5 %operands.1 = (bf16[112,56,128]{2,1,0:T(8,128)(2,1)}, bf16[256,56,128]{2,1,0:T(8,128)(2,1)}) custom-call(bf16[112,56,128]{2,1,0:T(8,128)(2,1)} %pair_ref.1, f32[56,128]{1,0:T(8,128)} %pad.4.mask_ref, f32[1,1,128]{2,1,0:T(1,128)} %bitcast.23, bf16[256,128]{1,0:T(8,128)(2,1)} %bitcast.18, bf16[256,128]{1,0:T(8,128)(2,1)} %bitcast.19), custom_call_target="tpu_custom_call" | custom-call | tf_op jit(solution)/shard_map/operands/pallas_call | solution.py:165
  12.4 0.0 copy-start.1
  12.4 0.0 copy-start
  12.4 126.3 %exchange.1 = bf16[4,32,56,128]{3,2,1,0:T(8,128)(2,1)} custom-call(bf16[4,32,2,56,128]{4,3,2,1,0:T(8,128)(2,1)} %bitcast.16), custom_call_target="tpu_custom_call" | custom-call | tf_op jit(solution)/shard_map/exchange/pallas_call | solution.py:176
  138.6 0.0 copy-done.1
  138.7 0.1 reshape.33
  138.8 0.1 copy.15
  138.8 0.8 reshape.37.gain_ref
  139.6 0.0 copy-done
  139.6 0.6 copy.16
  140.2 7.1 %update.1 = bf16[112,56,128]{2,1,0:T(8,128)(2,1)} custom-call(bf16[128,56,128]{2,1,0:T(8,128)(2,1)} %bitcast.15, bf16[112,56,128]{2,1,0:T(8,128)(2,1)} %get-tuple-element.8.normed_ref, f32[128,1,1]{2,1,0:T(1,128)} %reshape.37.gain_ref, bf16[128,128]{1,0:T(8,128)(2,1)} %gate_ref.1, bf16[128,128]{1,0:T(8,128)(2,1)} %bitcast.20), custom_call_target="tpu_custom_call" | custom-call | tf_op jit(solution)/shard_map/update/pallas_call | solution.py:191
  (1 shorter events, 0.0 us)
Async XLA Ops:
  12.4 126.3 %copy-start.1 = (f32[128]{0:T(128)S(1)}, f32[128]{0:T(128)}, u32[]{:S(2)}) copy-start(f32[128]{0:T(128)} %param.12) | copy-start | bytes 1540
  12.4 127.3 %copy-start = (bf16[128,128]{1,0:T(8,128)(2,1)S(1)}, bf16[128,128]{1,0:T(8,128)(2,1)}, u32[]{:S(2)}) copy-start(bf16[128,128]{1,0:T(8,128)(2,1)} %param.13) | copy-start | bytes 98308

commit v3 on v2

v3 whole, which is shorter than its diff:
```python
import functools

import jax
import jax.numpy as jnp
from jax import lax
from jax.experimental import pallas as pl
from jax.experimental.pallas import tpu as pltpu
from jax.sharding import PartitionSpec as P

EPS = 1e-05
LANES = 128
HALVES = 2
VMEM_LIMIT = 56 * 1024 * 1024
VMEM = pl.BlockSpec(memory_space=pltpu.VMEM)
ANY = pl.BlockSpec(memory_space=pl.ANY)


def chunks(length, size):
    return [(at, min(at + size, length)) for at in range(0, length, size)]


def pad_rows(values, to):
    short = to - values.shape[-2]
    if short == 0:
        return values
    shape = values.shape[:-2] + (short, values.shape[-1])
    return jnp.concatenate([values, jnp.zeros(shape, values.dtype)], axis=-2)


def layer_norm(values, gain, axis):
    middle = jnp.mean(values, axis=axis, keepdims=True)
    centred = values - middle
    spread = jnp.mean(centred * centred, axis=axis, keepdims=True)
    return centred * lax.rsqrt(spread + EPS) * gain


def operands_kernel(pair_ref, mask_ref, gain_ref, gates_ref, values_ref, normed_ref, out_ref):
    cols, padded = out_ref.shape[1], out_ref.shape[2]
    for low, high in chunks(cols, 8):
        normed = layer_norm(pair_ref[:, low:high, :].astype(jnp.float32), gain_ref[...], -1)
        normed_ref[:, low:high, :] = normed.astype(jnp.bfloat16)
        turned = pad_rows(jnp.transpose(normed, (1, 0, 2)), padded).astype(jnp.bfloat16)
        mine = []
        for at in range(high - low):
            turn = (((1,), (1,)), ((), ()))
            gates = lax.dot_general(gates_ref[...], turned[at], turn, preferred_element_type=jnp.float32)
            values = lax.dot_general(values_ref[...], turned[at], turn, preferred_element_type=jnp.float32)
            mine.append(jax.nn.sigmoid(gates) * values * mask_ref[low + at : low + at + 1, :])
        out_ref[:, low:high, :] = jnp.transpose(jnp.stack(mine), (1, 0, 2)).astype(jnp.bfloat16)


def exchange_kernel(
    n_row, n_col, rows, send_ref, out_ref, left, right, product,
    left_sent, left_came, right_sent, right_came, back_sent, back_came, own_left, own_right, own_back,
):
    steps, _, per, cols, padded = left.shape
    wide = n_col // HALVES
    owners = n_row * wide
    devices = n_row * n_col
    row, col = lax.axis_index("row"), lax.axis_index("col")
    half, spot = col // wide, lax.rem(col, wide)
    me, mine = row * n_col + col, row * wide + spot

    def anywhere(offset):
        other = lax.rem(me + offset, devices)
        to_row, to_col = other // n_col, lax.rem(other, n_col)
        return to_row * wide + lax.rem(to_col, wide), (to_row, to_col)

    def in_half(offset):
        other = lax.rem(mine + offset, owners)
        return other, (other // wide, half * wide + lax.rem(other, wide))

    barrier = pltpu.get_barrier_semaphore()

    def greet(offset, carry):
        pl.semaphore_signal(barrier, inc=1, device_id=anywhere(offset)[1], device_id_type=pl.DeviceIdType.MESH)
        return carry

    lax.fori_loop(1, devices, greet, 0)
    pl.semaphore_wait(barrier, devices - 1)

    def spread(count, place, source, target, sent, came):
        def one(offset, carry):
            other, device = place(offset)
            pltpu.make_async_remote_copy(
                src_ref=source.at[other],
                dst_ref=target,
                send_sem=sent,
                recv_sem=came,
                device_id=device,
                device_id_type=pl.DeviceIdType.MESH,
            ).start()
            return carry

        lax.fori_loop(1, count, one, 0)

    def own(h):
        return (
            pltpu.make_async_copy(send_ref.at[0, h, mine], left.at[h, me], own_left.at[h]),
            pltpu.make_async_copy(send_ref.at[1, h, mine], right.at[h, mine], own_right.at[h]),
        )

    def send(h, carry):
        for copy in own(h):
            copy.start()
        spread(devices, anywhere, send_ref.at[0, h], left.at[h, me], left_sent.at[h], left_came.at[h])
        spread(owners, in_half, send_ref.at[1, h], right.at[h, mine], right_sent.at[h], right_came.at[h])
        return carry

    lax.fori_loop(0, steps, send, 0)

    def wait_others(ref, count, sem):
        some = ref.at[pl.ds(0, count - 1)]
        pltpu.make_async_copy(some, some, sem).wait()

    def whole(held, h, p, width):
        pieces = [held[h, at * width : (at + 1) * width, p].reshape(width * cols, padded) for at in range(n_row)]
        return jnp.concatenate(pieces, axis=1)

    def own_result(h):
        return pltpu.make_async_copy(product.at[h, mine], out_ref.at[h, mine], own_back.at[h])

    def channels(h, carry):
        wait_others(left.at[h], devices, left_came.at[h])
        wait_others(right.at[h], owners, right_came.at[h])
        for copy in own(h):
            copy.wait()
        for p in range(per):
            firsts, seconds = whole(left, h, p, n_col), whole(right, h, p, wide)
            for at in range(n_row):
                panel = pad_rows(firsts[at * rows : (at + 1) * rows], padded)
                tri = lax.dot_general(seconds, panel, (((1,), (1,)), ((), ())), preferred_element_type=jnp.float32)
                product[h, at * wide : (at + 1) * wide, p] = tri.reshape(wide, cols, padded).astype(jnp.bfloat16)
        own_result(h).start()
        spread(owners, in_half, product.at[h], out_ref.at[h, mine], back_sent.at[h], back_came.at[h])
        return carry

    lax.fori_loop(0, steps, channels, 0)

    def finish(h, carry):
        wait_others(out_ref.at[h], owners, back_came.at[h])
        own_result(h).wait()
        wait_others(left.at[h], devices, left_sent.at[h])
        wait_others(right.at[h], owners, right_sent.at[h])
        wait_others(product.at[h], owners, back_sent.at[h])
        return carry

    lax.fori_loop(0, steps, finish, 0)


def update_kernel(tri_ref, normed_ref, gain_ref, gate_ref, weight_ref, out_ref):
    rows, cols, channels = normed_ref.shape
    for low, high in chunks(cols, 8):
        tri = layer_norm(tri_ref[:, low:high, :].astype(jnp.float32), gain_ref[...], 0)
        tri = jnp.transpose(tri, (1, 0, 2)).astype(jnp.bfloat16)
        mixed = []
        for at in range(high - low):
            turn = (((0,), (0,)), ((), ()))
            mixed.append(lax.dot_general(tri[at], weight_ref[...], turn, preferred_element_type=jnp.float32)[:rows])
        mixed = jnp.transpose(jnp.stack(mixed), (1, 0, 2))
        normed = normed_ref[:, low:high, :].astype(jnp.float32).reshape(rows * (high - low), channels)
        gate = jnp.dot(normed.astype(jnp.bfloat16), gate_ref[...], preferred_element_type=jnp.float32)
        gate = jax.nn.sigmoid(gate).reshape(rows, high - low, channels)
        out_ref[:, low:high, :] = (gate * mixed).astype(jnp.bfloat16)


def shards(pair, pair_mask, ln_in_gain, proj_ab, gate_weight, ln_out_gain, out_weight):
    rows, cols, channels = pair.shape
    hidden = out_weight.shape[0]
    n_row, n_col = lax.axis_size("row"), lax.axis_size("col")
    devices = n_row * n_col
    owners = devices // HALVES
    part = hidden // owners
    per = min(part, 2)
    steps = part // per
    padded = -(-rows // LANES) * LANES
    plain = pltpu.CompilerParams(vmem_limit_bytes=VMEM_LIMIT)
    columns = proj_ab.reshape(channels, 2, 2, owners, steps, per).transpose(2, 1, 4, 3, 5, 0)
    columns = columns.reshape(2, 2 * hidden, channels)
    weight = jnp.pad(pair_mask.astype(jnp.float32).T, ((0, 0), (0, padded - rows)))
    normed, operands = pl.pallas_call(
        operands_kernel,
        out_shape=(
            jax.ShapeDtypeStruct((rows, cols, channels), jnp.bfloat16),
            jax.ShapeDtypeStruct((2 * hidden, cols, padded), jnp.bfloat16),
        ),
        in_specs=[VMEM] * 5,
        out_specs=(VMEM, VMEM),
        compiler_params=plain,
        name="operands",
    )(pair, weight, ln_in_gain.reshape(1, 1, channels), columns[0], columns[1])
    tri = pl.pallas_call(
        functools.partial(exchange_kernel, n_row, n_col, rows),
        out_shape=jax.ShapeDtypeStruct((steps, owners, per, cols, padded), jnp.bfloat16),
        in_specs=[ANY],
        out_specs=ANY,
        scratch_shapes=[
            pltpu.VMEM((steps, devices, per, cols, padded), jnp.bfloat16),
            pltpu.VMEM((steps, owners, per, cols, padded), jnp.bfloat16),
            pltpu.VMEM((steps, owners, per, cols, padded), jnp.bfloat16),
        ]
        + [pltpu.SemaphoreType.DMA((steps,))] * 9,
        compiler_params=pltpu.CompilerParams(collective_id=0, has_side_effects=True, vmem_limit_bytes=VMEM_LIMIT),
        name="exchange",
    )(operands.reshape(2, steps, owners, per, cols, padded))
    gain = ln_out_gain.reshape(owners, steps, per).transpose(1, 0, 2).reshape(hidden, 1, 1)
    mixing = out_weight.reshape(owners, steps, per, channels).transpose(1, 0, 2, 3).reshape(hidden, channels)
    return pl.pallas_call(
        update_kernel,
        out_shape=jax.ShapeDtypeStruct((rows, cols, channels), jnp.bfloat16),
        in_specs=[VMEM] * 5,
        out_specs=VMEM,
        compiler_params=plain,
        name="update",
    )(tri.reshape(hidden, cols, padded), normed, gain, gate_weight, mixing)


def solution(mesh):
    in_specs = (P("row", "col", None), P("row", "col"), P(), P(), P(), P(), P())
    out_specs = P("row", "col", None)
    return jax.shard_map(shards, mesh=mesh, in_specs=in_specs, out_specs=out_specs, check_vma=False)
```

time: 148 us -> 130 us (0.88)
  Pallas kernels: 142 us -> 124 us
    pallas_call x1, Pallas kernels: 126 us -> 109 us  [shards(): pl.pallas_call(functools.partial(exchange_kernel, n_row, n_col, rows), ou...]
where the time goes in v3:
time: 130 us
  Pallas kernels  124 us (95%)
  local copies, waits for them, and re-layouts  4.57 us (4%)
    pallas_call x1, Pallas kernels, shards(): pl.pallas_call(functools.partial(exchange_kernel, n_row, n_col, rows), ou...  109 us
    pallas_call x1, Pallas kernels, shards(): pl.pallas_call(operands_kernel, out_shape=(jax.ShapeDtypeStruct((rows, co...  8.54 us
    pallas_call x1, Pallas kernels, shards(): pl.pallas_call(update_kernel, out_shape=jax.ShapeDtypeStruct((rows, cols,...  7.14 us

profile of v3, /device:TPU:0, one launch (start us, length us, event | category | flops | bytes accessed | tf_op | source)
XLA Modules:
  0.0 129.6 jit_solution(9022846603753176375)
XLA Ops:
  0.0 1.0 copy.12
  1.0 0.1 fusion
  1.1 0.7 copy.13
  1.8 0.7 copy.14
  2.5 0.8 convert_bitcast_fusion
  3.2 0.6 pad.4.mask_ref
  3.8 8.5 %operands.1 = (bf16[112,56,128]{2,1,0:T(8,128)(2,1)}, bf16[256,56,128]{2,1,0:T(8,128)(2,1)}) custom-call(bf16[112,56,128]{2,1,0:T(8,128)(2,1)} %pair_ref.1, f32[56,128]{1,0:T(8,128)} %pad.4.mask_ref, f32[1,1,128]{2,1,0:T(1,128)} %bitcast.23, bf16[256,128]{1,0:T(8,128)(2,1)} %bitcast.18, bf16[256,128]{1,0:T(8,128)(2,1)} %bitcast.19), custom_call_target="tpu_custom_call" | custom-call | tf_op jit(solution)/shard_map/operands/pallas_call | solution.py:181
  12.4 0.0 copy-start.1
  12.4 0.0 copy-start
  12.4 108.6 %exchange.1 = bf16[4,16,2,56,128]{4,3,2,1,0:T(8,128)(2,1)} custom-call(bf16[2,4,16,2,56,128]{5,4,3,2,1,0:T(8,128)(2,1)} %bitcast.16), custom_call_target="tpu_custom_call" | custom-call | tf_op jit(solution)/shard_map/exchange/pallas_call | solution.py:192
  121.0 0.0 copy-done.1
  121.0 0.2 reshape.33
  121.1 0.7 reshape.37.gain_ref
  121.9 0.0 copy-done
  121.9 0.6 copy.16
  122.5 7.1 %update.1 = bf16[112,56,128]{2,1,0:T(8,128)(2,1)} custom-call(bf16[128,56,128]{2,1,0:T(8,128)(2,1)} %bitcast.15, bf16[112,56,128]{2,1,0:T(8,128)(2,1)} %get-tuple-element.8.normed_ref, f32[128,1,1]{2,1,0:T(1,128)} %reshape.37.gain_ref, bf16[128,128]{1,0:T(8,128)(2,1)} %gate_ref.1, bf16[128,128]{1,0:T(8,128)(2,1)} %bitcast.20), custom_call_target="tpu_custom_call" | custom-call | tf_op jit(solution)/shard_map/update/pallas_call | solution.py:208
  (1 shorter events, 0.0 us)
Async XLA Ops:
  12.4 108.6 %copy-start.1 = (f32[128]{0:T(128)S(1)}, f32[128]{0:T(128)}, u32[]{:S(2)}) copy-start(f32[128]{0:T(128)} %param.12) | copy-start | bytes 1540
  12.4 109.5 %copy-start = (bf16[128,128]{1,0:T(8,128)(2,1)S(1)}, bf16[128,128]{1,0:T(8,128)(2,1)}, u32[]{:S(2)}) copy-start(bf16[128,128]{1,0:T(8,128)(2,1)} %param.13) | copy-start | bytes 98308

commit v4 on v3

--- a/solution.py
+++ b/solution.py
@@ -9,7 +9,6 @@
 
 EPS = 1e-05
 LANES = 128
-HALVES = 2
 VMEM_LIMIT = 56 * 1024 * 1024
 VMEM = pl.BlockSpec(memory_space=pltpu.VMEM)
 ANY = pl.BlockSpec(memory_space=pl.ANY)
@@ -50,102 +49,163 @@
 
 
 def exchange_kernel(
-    n_row, n_col, rows, send_ref, out_ref, left, right, product,
-    left_sent, left_came, right_sent, right_came, back_sent, back_came, own_left, own_right, own_back,
+    n_row, n_col, rows, ends, send_ref, out_ref, left, right, product,
+    left_sent, left_came, far_sent, far_came, relay_sent, right_sent, right_came, back_sent, back_came,
 ):
-    steps, _, per, cols, padded = left.shape
-    wide = n_col // HALVES
-    owners = n_row * wide
+    steps, _, fellows, per, cols, padded = left.shape
+    wide, quarter = n_col // 2, n_col // 4
+    owners = n_row * quarter
     devices = n_row * n_col
     row, col = lax.axis_index("row"), lax.axis_index("col")
     half, spot = col // wide, lax.rem(col, wide)
-    me, mine = row * n_col + col, row * wide + spot
-
-    def anywhere(offset):
-        other = lax.rem(me + offset, devices)
-        to_row, to_col = other // n_col, lax.rem(other, n_col)
-        return to_row * wide + lax.rem(to_col, wide), (to_row, to_col)
-
-    def in_half(offset):
-        other = lax.rem(mine + offset, owners)
-        return other, (other // wide, half * wide + lax.rem(other, wide))
+    place, seat = spot // quarter, lax.rem(spot, quarter)
+    middle = lax.rem(place + half, 2)
+    mine, me = row * wide + spot, row * quarter + seat
+
+    def owner_at(other, in_half, to_middle):
+        shift = lax.rem(in_half + to_middle, 2) * quarter
+        return other // quarter, in_half * wide + shift + lax.rem(other, quarter)
 
     barrier = pltpu.get_barrier_semaphore()
 
     def greet(offset, carry):
-        pl.semaphore_signal(barrier, inc=1, device_id=anywhere(offset)[1], device_id_type=pl.DeviceIdType.MESH)
+        other = lax.rem(row * n_col + col + offset, devices)
+        device = other // n_col, lax.rem(other, n_col)
+        pl.semaphore_signal(barrier, inc=1, device_id=device, device_id_type=pl.DeviceIdType.MESH)
         return carry
 
     lax.fori_loop(1, devices, greet, 0)
     pl.semaphore_wait(barrier, devices - 1)
 
-    def spread(count, place, source, target, sent, came):
+    def remote(source, target, sent, came, device):
+        return pltpu.make_async_remote_copy(
+            src_ref=source,
+            dst_ref=target,
+            send_sem=sent,
+            recv_sem=came,
+            device_id=device,
+            device_id_type=pl.DeviceIdType.MESH,
+        )
+
+    def to_owners(source, target, sent, came, in_half, to_middle, skip):
         def one(offset, carry):
-            other, device = place(offset)
-            pltpu.make_async_remote_copy(
-                src_ref=source.at[other],
-                dst_ref=target,
-                send_sem=sent,
-                recv_sem=came,
-                device_id=device,
-                device_id_type=pl.DeviceIdType.MESH,
-            ).start()
-            return carry
-
-        lax.fori_loop(1, count, one, 0)
-
-    def own(h):
-        return (
-            pltpu.make_async_copy(send_ref.at[0, h, mine], left.at[h, me], own_left.at[h]),
-            pltpu.make_async_copy(send_ref.at[1, h, mine], right.at[h, mine], own_right.at[h]),
+            other = lax.rem(me + offset, owners)
+            remote(source.at[other], target, sent, came, owner_at(other, in_half, to_middle)).start()
+            return carry
+
+        lax.fori_loop(skip, owners, one, 0)
+
+    def belongs(h):
+        return middle if h >= ends else 1 - middle
+
+    def send(side, h):
+        target, sent, came = (left.at[h, half], left_sent, left_came) if side == 0 else (right.at[h], right_sent, right_came)
+        member = belongs(h)
+
+        @pl.when(member == 1)
+        def _():
+            pltpu.make_async_copy(send_ref.at[side, h, me], target.at[mine], came.at[h]).start()
+
+        to_owners(send_ref.at[side, h], target.at[mine], sent.at[h], came.at[h], half, int(h >= ends), member)
+
+    def send_far(h):
+        to_owners(send_ref.at[0, h], left.at[h, half, mine], far_sent.at[h], far_came.at[h], 1 - half, 0, 0)
+
+    send(0, ends)
+    for h in range(ends):
+        send_far(h)
+        send(0, h)
+        send(1, h)
+    for h in range(ends, steps):
+        if h > ends:
+            send(0, h)
+        send(1, h)
+
+    def wait_for(ref, sem):
+        pltpu.make_async_copy(ref, ref, sem).wait()
+
+    def relay(h):
+        return remote(
+            left.at[h, half], left.at[h, half], relay_sent.at[h], far_came.at[h], (row, owner_at(me, 1 - half, 1)[1])
         )
 
-    def send(h, carry):
-        for copy in own(h):
-            copy.start()
-        spread(devices, anywhere, send_ref.at[0, h], left.at[h, me], left_sent.at[h], left_came.at[h])
-        spread(owners, in_half, send_ref.at[1, h], right.at[h, mine], right_sent.at[h], right_came.at[h])
-        return carry
-
-    lax.fori_loop(0, steps, send, 0)
-
-    def wait_others(ref, count, sem):
-        some = ref.at[pl.ds(0, count - 1)]
-        pltpu.make_async_copy(some, some, sem).wait()
-
-    def whole(held, h, p, width):
-        pieces = [held[h, at * width : (at + 1) * width, p].reshape(width * cols, padded) for at in range(n_row)]
-        return jnp.concatenate(pieces, axis=1)
-
-    def own_result(h):
-        return pltpu.make_async_copy(product.at[h, mine], out_ref.at[h, mine], own_back.at[h])
-
-    def channels(h, carry):
-        wait_others(left.at[h], devices, left_came.at[h])
-        wait_others(right.at[h], owners, right_came.at[h])
-        for copy in own(h):
-            copy.wait()
+    def pass_on(h):
+        wait_for(left.at[h, half], left_came.at[h])
+        relay(h).start()
+
+    def channels(h):
+        wait_for(right.at[h], right_came.at[h])
+        wait_for(left.at[h, 1 - half], far_came.at[h])
         for p in range(per):
-            firsts, seconds = whole(left, h, p, n_col), whole(right, h, p, wide)
+            firsts, seconds = [], []
+            for at in range(n_row):
+                span = slice(at * wide, (at + 1) * wide)
+                both = [left[h, side, span, p].reshape(wide * cols, padded) for side in range(2)]
+                firsts.append(jnp.concatenate(both, axis=0))
+                seconds.append(right[h, span, p].reshape(wide * cols, padded))
+            firsts, seconds = jnp.concatenate(firsts, axis=1), jnp.concatenate(seconds, axis=1)
             for at in range(n_row):
                 panel = pad_rows(firsts[at * rows : (at + 1) * rows], padded)
                 tri = lax.dot_general(seconds, panel, (((1,), (1,)), ((), ())), preferred_element_type=jnp.float32)
                 product[h, at * wide : (at + 1) * wide, p] = tri.reshape(wide, cols, padded).astype(jnp.bfloat16)
-        own_result(h).start()
-        spread(owners, in_half, product.at[h], out_ref.at[h, mine], back_sent.at[h], back_came.at[h])
-        return carry
-
-    lax.fori_loop(0, steps, channels, 0)
-
-    def finish(h, carry):
-        wait_others(out_ref.at[h], owners, back_came.at[h])
-        own_result(h).wait()
-        wait_others(left.at[h], devices, left_sent.at[h])
-        wait_others(right.at[h], owners, right_sent.at[h])
-        wait_others(product.at[h], owners, back_sent.at[h])
-        return carry
-
-    lax.fori_loop(0, steps, finish, 0)
+        pltpu.make_async_copy(product.at[h, mine], out_ref.at[h, me], back_came.at[h]).start()
+
+        def one(offset, carry):
+            other = lax.rem(mine + offset, fellows)
+            device = other // wide, half * wide + lax.rem(other, wide)
+            remote(product.at[h, other], out_ref.at[h, me], back_sent.at[h], back_came.at[h], device).start()
+            return carry
+
+        lax.fori_loop(1, fellows, one, 0)
+
+    ahead = min(3, steps - ends)
+
+    @pl.when(middle == 1)
+    def _():
+        for h in range(ends, ends + ahead):
+            pass_on(h)
+
+        def one(h, carry):
+            pass_on(h + ahead)
+            channels(h)
+            return carry
+
+        def last(h, carry):
+            channels(h)
+            return carry
+
+        lax.fori_loop(ends, steps - ahead, one, 0)
+        lax.fori_loop(steps - ahead, steps, last, 0)
+
+    @pl.when(middle == 0)
+    def _():
+        def one(h, carry):
+            wait_for(left.at[h, half], left_came.at[h])
+            channels(h)
+            return carry
+
+        lax.fori_loop(0, ends, one, 0)
+
+    for h in range(steps):
+        member = belongs(h)
+        wait_for(out_ref.at[h], back_came.at[h])
+        if h < ends:
+            wait_for(left.at[h, 0, pl.ds(0, owners)], far_sent.at[h])
+
+        @pl.when(member == 1)
+        def _():
+            others = left.at[h, 0, pl.ds(0, owners - 1)]
+            wait_for(others, left_sent.at[h])
+            wait_for(others, right_sent.at[h])
+            wait_for(product.at[h, pl.ds(0, fellows - 1)], back_sent.at[h])
+            if h >= ends:
+                wait_for(left.at[h, half], relay_sent.at[h])
+
+        @pl.when(member == 0)
+        def _():
+            everyone = left.at[h, 0, pl.ds(0, owners)]
+            wait_for(everyone, left_sent.at[h])
+            wait_for(everyone, right_sent.at[h])
 
 
 def update_kernel(tri_ref, normed_ref, gain_ref, gate_ref, weight_ref, out_ref):
@@ -168,11 +228,12 @@
     rows, cols, channels = pair.shape
     hidden = out_weight.shape[0]
     n_row, n_col = lax.axis_size("row"), lax.axis_size("col")
-    devices = n_row * n_col
-    owners = devices // HALVES
+    fellows = n_row * (n_col // 2)
+    owners = n_row * (n_col // 4)
     part = hidden // owners
-    per = min(part, 2)
+    per = max(part // 8, 1)
     steps = part // per
+    ends = steps // 4
     padded = -(-rows // LANES) * LANES
     plain = pltpu.CompilerParams(vmem_limit_bytes=VMEM_LIMIT)
     columns = proj_ab.reshape(channels, 2, 2, owners, steps, per).transpose(2, 1, 4, 3, 5, 0)
@@ -190,14 +251,14 @@
         name="operands",
     )(pair, weight, ln_in_gain.reshape(1, 1, channels), columns[0], columns[1])
     tri = pl.pallas_call(
-        functools.partial(exchange_kernel, n_row, n_col, rows),
+        functools.partial(exchange_kernel, n_row, n_col, rows, ends),
         out_shape=jax.ShapeDtypeStruct((steps, owners, per, cols, padded), jnp.bfloat16),
         in_specs=[ANY],
         out_specs=ANY,
         scratch_shapes=[
-            pltpu.VMEM((steps, devices, per, cols, padded), jnp.bfloat16),
-            pltpu.VMEM((steps, owners, per, cols, padded), jnp.bfloat16),
-            pltpu.VMEM((steps, owners, per, cols, padded), jnp.bfloat16),
+            pltpu.VMEM((steps, 2, fellows, per, cols, padded), jnp.bfloat16),
+            pltpu.VMEM((steps, fellows, per, cols, padded), jnp.bfloat16),
+            pltpu.VMEM((steps, fellows, per, cols, padded), jnp.bfloat16),
         ]
         + [pltpu.SemaphoreType.DMA((steps,))] * 9,
         compiler_params=pltpu.CompilerParams(collective_id=0, has_side_effects=True, vmem_limit_bytes=VMEM_LIMIT),

time: 130 us -> 118 us (0.908)
  Pallas kernels: 124 us -> 112 us
    pallas_call x1, Pallas kernels: 109 us -> 96.8 us  [shards(): pl.pallas_call(functools.partial(exchange_kernel, n_row, n_col, rows, end...]
where the time goes in v4:
time: 118 us
  Pallas kernels  112 us (95%)
  local copies, waits for them, and re-layouts  4.54 us (4%)
    pallas_call x1, Pallas kernels, shards(): pl.pallas_call(functools.partial(exchange_kernel, n_row, n_col, rows, end...  96.8 us
    pallas_call x1, Pallas kernels, shards(): pl.pallas_call(operands_kernel, out_shape=(jax.ShapeDtypeStruct((rows, co...  8.54 us
    pallas_call x1, Pallas kernels, shards(): pl.pallas_call(update_kernel, out_shape=jax.ShapeDtypeStruct((rows, cols,...  7.14 us

profile of v4, /device:TPU:0, one launch (start us, length us, event | category | flops | bytes accessed | tf_op | source)
XLA Modules:
  0.0 117.8 jit_solution(690436356586369203)
XLA Ops:
  0.0 1.0 copy.12
  1.0 0.1 fusion
  1.1 0.7 copy.13
  1.8 0.7 copy.14
  2.5 0.8 convert_bitcast_fusion
  3.2 0.6 pad.4.mask_ref
  3.8 8.5 %operands.1 = (bf16[112,56,128]{2,1,0:T(8,128)(2,1)}, bf16[256,56,128]{2,1,0:T(8,128)(2,1)}) custom-call(bf16[112,56,128]{2,1,0:T(8,128)(2,1)} %pair_ref.1, f32[56,128]{1,0:T(8,128)} %pad.4.mask_ref, f32[1,1,128]{2,1,0:T(1,128)} %bitcast.23, bf16[256,128]{1,0:T(8,128)(2,1)} %bitcast.18, bf16[256,128]{1,0:T(8,128)(2,1)} %bitcast.19), custom_call_target="tpu_custom_call" | custom-call | tf_op jit(solution)/shard_map/operands/pallas_call | solution.py:242
  12.4 0.0 copy-start.1
  12.4 0.0 copy-start
  12.4 96.8 %exchange.1 = bf16[8,8,2,56,128]{4,3,2,1,0:T(8,128)(2,1)} custom-call(bf16[2,8,8,2,56,128]{5,4,3,2,1,0:T(8,128)(2,1)} %bitcast.16), custom_call_target="tpu_custom_call" | custom-call | tf_op jit(solution)/shard_map/exchange/pallas_call | solution.py:253
  109.2 0.0 copy-done.1
  109.2 0.1 reshape.33
  109.3 0.7 reshape.37.gain_ref
  110.1 0.0 copy-done
  110.1 0.6 copy.16
  110.7 7.1 %update.1 = bf16[112,56,128]{2,1,0:T(8,128)(2,1)} custom-call(bf16[128,56,128]{2,1,0:T(8,128)(2,1)} %bitcast.15, bf16[112,56,128]{2,1,0:T(8,128)(2,1)} %get-tuple-element.8.normed_ref, f32[128,1,1]{2,1,0:T(1,128)} %reshape.37.gain_ref, bf16[128,128]{1,0:T(8,128)(2,1)} %gate_ref.1, bf16[128,128]{1,0:T(8,128)(2,1)} %bitcast.20), custom_call_target="tpu_custom_call" | custom-call | tf_op jit(solution)/shard_map/update/pallas_call | solution.py:269
  (1 shorter events, 0.0 us)
Async XLA Ops:
  12.4 96.8 %copy-start.1 = (f32[128]{0:T(128)S(1)}, f32[128]{0:T(128)}, u32[]{:S(2)}) copy-start(f32[128]{0:T(128)} %param.12) | copy-start | bytes 1540
  12.4 97.7 %copy-start = (bf16[128,128]{1,0:T(8,128)(2,1)S(1)}, bf16[128,128]{1,0:T(8,128)(2,1)}, u32[]{:S(2)}) copy-start(bf16[128,128]{1,0:T(8,128)(2,1)} %param.13) | copy-start | bytes 98308

commit v5 on v4

v5 whole, which is shorter than its diff:
```python
import functools

import jax
import jax.numpy as jnp
from jax import lax
from jax.experimental import pallas as pl
from jax.experimental.pallas import tpu as pltpu
from jax.sharding import PartitionSpec as P

EPS = 1e-05
LANES = 128
VMEM_LIMIT = 56 * 1024 * 1024
VMEM = pl.BlockSpec(memory_space=pltpu.VMEM)


def chunks(length, size):
    return [(at, min(at + size, length)) for at in range(0, length, size)]


def pad_rows(values, to):
    short = to - values.shape[-2]
    if short == 0:
        return values
    shape = values.shape[:-2] + (short, values.shape[-1])
    return jnp.concatenate([values, jnp.zeros(shape, values.dtype)], axis=-2)


def layer_norm(values, gain, axis):
    middle = jnp.mean(values, axis=axis, keepdims=True)
    centred = values - middle
    spread = jnp.mean(centred * centred, axis=axis, keepdims=True)
    return centred * lax.rsqrt(spread + EPS) * gain


def triangle_kernel(
    n_row, n_col, ends, pair_ref, mask_ref, in_gain_ref, proj_ref, gate_ref, out_gain_ref, weight_ref, update_ref,
    turned, gates, operands, left, right, product, landed, left_sent, left_came, far_sent, far_came, relay_sent, right_sent, right_came, back_sent, back_came,
):
    steps, _, fellows, per, cols, padded = left.shape
    rows, channels = pair_ref.shape[0], pair_ref.shape[2]
    hidden = weight_ref.shape[0]
    wide, quarter = n_col // 2, n_col // 4
    owners = n_row * quarter
    devices = n_row * n_col
    row, col = lax.axis_index("row"), lax.axis_index("col")
    half, spot = col // wide, lax.rem(col, wide)
    place, seat = spot // quarter, lax.rem(spot, quarter)
    middle = lax.rem(place + half, 2)
    mine, me = row * wide + spot, row * quarter + seat

    def owner_at(other, in_half, to_middle):
        shift = lax.rem(in_half + to_middle, 2) * quarter
        return other // quarter, in_half * wide + shift + lax.rem(other, quarter)

    barrier = pltpu.get_barrier_semaphore()

    def greet(offset, carry):
        other = lax.rem(row * n_col + col + offset, devices)
        device = other // n_col, lax.rem(other, n_col)
        pl.semaphore_signal(barrier, inc=1, device_id=device, device_id_type=pl.DeviceIdType.MESH)
        return carry

    lax.fori_loop(1, devices, greet, 0)

    for low, high in chunks(cols, 8):
        normed = layer_norm(pair_ref[:, low:high, :].astype(jnp.float32), in_gain_ref[...], -1)
        turned[low:high] = pad_rows(jnp.transpose(normed, (1, 0, 2)), padded).astype(jnp.bfloat16)

    def make(side):
        weights = jnp.transpose(proj_ref[:, side * 2 * hidden : (side + 1) * 2 * hidden].astype(jnp.float32))
        weights = weights.astype(jnp.bfloat16)
        for low, high in chunks(cols, 8):
            rest = jnp.zeros((high - low, padded - rows), jnp.float32)
            valid = jnp.concatenate([mask_ref[low:high, :].astype(jnp.float32), rest], axis=1)
            each = []
            for at in range(low, high):
                projected = lax.dot_general(
                    weights, turned[at], (((1,), (1,)), ((), ())), preferred_element_type=jnp.float32
                )
                each.append(jax.nn.sigmoid(projected[:hidden]) * projected[hidden:] * valid[at - low : at - low + 1])
            each = jnp.transpose(jnp.stack(each), (1, 0, 2)).astype(jnp.bfloat16)
            operands[side, :, :, :, low:high, :] = each.reshape(owners, steps, per, high - low, padded)

    make(0)
    pl.semaphore_wait(barrier, devices - 1)

    def remote(source, target, sent, came, device):
        return pltpu.make_async_remote_copy(
            src_ref=source,
            dst_ref=target,
            send_sem=sent,
            recv_sem=came,
            device_id=device,
            device_id_type=pl.DeviceIdType.MESH,
        )

    def to_owners(source, target, sent, came, in_half, to_middle, skip):
        def one(offset, carry):
            other = lax.rem(me + offset, owners)
            remote(source(other), target, sent, came, owner_at(other, in_half, to_middle)).start()
            return carry

        lax.fori_loop(skip, owners, one, 0)

    def belongs(h):
        return middle if h >= ends else 1 - middle

    def send(side, h):
        target, sent, came = (left.at[h, half], left_sent, left_came) if side == 0 else (right.at[h], right_sent, right_came)
        member = belongs(h)

        @pl.when(member == 1)
        def _():
            pltpu.make_async_copy(operands.at[side, me, h], target.at[mine], came.at[h]).start()

        to_owners(lambda other: operands.at[side, other, h], target.at[mine], sent.at[h], came.at[h], half, int(h >= ends), member)

    def send_far(h):
        target = left.at[h, half, mine]
        to_owners(lambda other: operands.at[0, other, h], target, far_sent.at[h], far_came.at[h], 1 - half, 0, 0)

    send(0, ends)
    for h in range(ends):
        send_far(h)
        send(0, h)
    for h in range(ends + 1, steps):
        send(0, h)
    make(1)
    for h in range(steps):
        send(1, h)

    def open_gate(at, carry):
        gate = jnp.dot(turned[at], gate_ref[...], preferred_element_type=jnp.float32)
        gates[at] = jax.nn.sigmoid(gate)
        return carry

    lax.fori_loop(0, cols, open_gate, 0)

    def wait_for(ref, sem):
        pltpu.make_async_copy(ref, ref, sem).wait()

    def relay(h):
        return remote(
            left.at[h, half], left.at[h, half], relay_sent.at[h], far_came.at[h], (row, owner_at(me, 1 - half, 1)[1])
        )

    def pass_on(h):
        wait_for(left.at[h, half], left_came.at[h])
        relay(h).start()

    def channels(h):
        wait_for(right.at[h], right_came.at[h])
        wait_for(left.at[h, 1 - half], far_came.at[h])
        for p in range(per):
            firsts, seconds = [], []
            for at in range(n_row):
                span = slice(at * wide, (at + 1) * wide)
                both = [left[h, side, span, p].reshape(wide * cols, padded) for side in range(2)]
                firsts.append(jnp.concatenate(both, axis=0))
                seconds.append(right[h, span, p].reshape(wide * cols, padded))
            firsts, seconds = jnp.concatenate(firsts, axis=1), jnp.concatenate(seconds, axis=1)
            for at in range(n_row):
                panel = pad_rows(firsts[at * rows : (at + 1) * rows], padded)
                tri = lax.dot_general(seconds, panel, (((1,), (1,)), ((), ())), preferred_element_type=jnp.float32)
                product[h, at * wide : (at + 1) * wide, p] = tri.reshape(wide, cols, padded).astype(jnp.bfloat16)
        pltpu.make_async_copy(product.at[h, mine], landed.at[me, h], back_came.at[h]).start()

        def one(offset, carry):
            other = lax.rem(mine + offset, fellows)
            device = other // wide, half * wide + lax.rem(other, wide)
            remote(product.at[h, other], landed.at[me, h], back_sent.at[h], back_came.at[h], device).start()
            return carry

        lax.fori_loop(1, fellows, one, 0)

    ahead = min(3, steps - ends)

    @pl.when(middle == 1)
    def _():
        for h in range(ends, ends + ahead):
            pass_on(h)

        def one(h, carry):
            pass_on(h + ahead)
            channels(h)
            return carry

        def last(h, carry):
            channels(h)
            return carry

        lax.fori_loop(ends, steps - ahead, one, 0)
        lax.fori_loop(steps - ahead, steps, last, 0)

    @pl.when(middle == 0)
    def _():
        def one(h, carry):
            wait_for(left.at[h, half], left_came.at[h])
            channels(h)
            return carry

        lax.fori_loop(0, ends, one, 0)

    for h in range(steps):
        member = belongs(h)
        wait_for(landed.at[:, h], back_came.at[h])
        if h < ends:
            wait_for(left.at[h, 0, pl.ds(0, owners)], far_sent.at[h])

        @pl.when(member == 1)
        def _():
            others = left.at[h, 0, pl.ds(0, owners - 1)]
            wait_for(others, left_sent.at[h])
            wait_for(others, right_sent.at[h])
            wait_for(product.at[h, pl.ds(0, fellows - 1)], back_sent.at[h])
            if h >= ends:
                wait_for(left.at[h, half], relay_sent.at[h])

        @pl.when(member == 0)
        def _():
            everyone = left.at[h, 0, pl.ds(0, owners)]
            wait_for(everyone, left_sent.at[h])
            wait_for(everyone, right_sent.at[h])

    for low, high in chunks(cols, 8):
        tri = landed[:, :, :, low:high, :].astype(jnp.float32).reshape(hidden, high - low, padded)
        tri = jnp.transpose(layer_norm(tri, out_gain_ref[...], 0), (1, 0, 2)).astype(jnp.bfloat16)
        mixed = []
        for at in range(low, high):
            mix = lax.dot_general(
                tri[at - low], weight_ref[...], (((0,), (0,)), ((), ())), preferred_element_type=jnp.float32
            )
            mixed.append((gates[at] * mix)[:rows])
        update_ref[:, low:high, :] = jnp.transpose(jnp.stack(mixed), (1, 0, 2)).astype(jnp.bfloat16)


def shards(pair, pair_mask, ln_in_gain, proj_ab, gate_weight, ln_out_gain, out_weight):
    rows, cols, channels = pair.shape
    hidden = out_weight.shape[0]
    n_row, n_col = lax.axis_size("row"), lax.axis_size("col")
    fellows = n_row * (n_col // 2)
    owners = n_row * (n_col // 4)
    part = hidden // owners
    per = max(part // 8, 1)
    steps = part // per
    ends = steps // 4
    padded = -(-rows // LANES) * LANES
    block = (per, cols, padded)
    return pl.pallas_call(
        functools.partial(triangle_kernel, n_row, n_col, ends),
        out_shape=jax.ShapeDtypeStruct((rows, cols, channels), jnp.bfloat16),
        in_specs=[VMEM] * 7,
        out_specs=VMEM,
        scratch_shapes=[
            pltpu.VMEM((cols, padded, channels), jnp.bfloat16),
            pltpu.VMEM((cols, padded, channels), jnp.float32),
            pltpu.VMEM((2, owners, steps) + block, jnp.bfloat16),
            pltpu.VMEM((steps, 2, fellows) + block, jnp.bfloat16),
            pltpu.VMEM((steps, fellows) + block, jnp.bfloat16),
            pltpu.VMEM((steps, fellows) + block, jnp.bfloat16),
            pltpu.VMEM((owners, steps) + block, jnp.bfloat16),
        ]
        + [pltpu.SemaphoreType.DMA((steps,))] * 9,
        compiler_params=pltpu.CompilerParams(collective_id=0, has_side_effects=True, vmem_limit_bytes=VMEM_LIMIT),
        name="triangle",
    )(
        pair,
        pair_mask.T,
        ln_in_gain.reshape(1, 1, channels),
        proj_ab,
        gate_weight,
        ln_out_gain.reshape(hidden, 1, 1),
        out_weight,
    )


def solution(mesh):
    in_specs = (P("row", "col", None), P("row", "col"), P(), P(), P(), P(), P())
    out_specs = P("row", "col", None)
    return jax.shard_map(shards, mesh=mesh, in_specs=in_specs, out_specs=out_specs, check_vma=False)
```

time: 118 us -> 105 us (0.89)
  Pallas kernels: 112 us -> 101 us
    pallas_call x3 -> x1, Pallas kernels: 112 us -> 101 us  [shards(): pl.pallas_call(functools.partial(triangle_kernel, n_row, n_col, ends), ou...]
    unnamed x5 -> x1, local copies, waits for them, and re-layouts: 1.03 us -> 2.7 us
    slice x3 -> x0, local copies, waits for them, and re-layouts: 1.42 us -> none  [the longest x2 0.75 us: shards(): columns[1]]
where the time goes in v5:
time: 105 us
  Pallas kernels  101 us (96%)
  local copies, waits for them, and re-layouts  4.09 us (4%)
    pallas_call x1, Pallas kernels, shards(): pl.pallas_call(functools.partial(triangle_kernel, n_row, n_col, ends), ou...  101 us
    unnamed x1, local copies, waits for them, and re-layouts  2.7 us

profile of v5, /device:TPU:0, one launch (start us, length us, event | category | flops | bytes accessed | tf_op | source)
XLA Modules:
  0.0 105.2 jit_solution(32249586662914510)
XLA Ops:
  0.0 1.4 %copy.8.out_gain_ref = f32[128,1,1]{2,1,0:T(1,128)} copy(f32[128,1,1]{0,2,1:T(1,128)} %bitcast.4) | data formatting | bytes 1024 | tf_op jit(solution)/shard_map/reshape | solution.py:272
  1.4 101.1 %triangle.1 = bf16[112,56,128]{2,1,0:T(8,128)(2,1)} custom-call(bf16[112,56,128]{2,1,0:T(8,128)(2,1)} %pair_ref.1, s32[56,112]{1,0:T(8,128)} %bitcast.3, f32[1,1,128]{2,1,0:T(1,128)} %bitcast.5, bf16[128,512]{1,0:T(8,128)(2,1)} %proj_ref.1, bf16[128,128]{1,0:T(8,128)(2,1)} %gate_ref.1, f32[128,1,1]{2,1,0:T(1,128)} %copy.8.out_gain_ref, ...), custom_call_target="tpu_custom_call" | custom-call | tf_op jit(solution)/shard_map/triangle/pallas_call | solution.py:249
  102.5 2.7 %copy.10 = bf16[112,56,128]{2,1,0:T(8,128)(2,1)} copy(bf16[112,56,128]{2,1,0:T(8,128)(2,1)} %triangle.1) | data formatting | bytes 3211264

commit v6 on v5

--- a/solution.py
+++ b/solution.py
@@ -25,11 +25,11 @@
     return jnp.concatenate([values, jnp.zeros(shape, values.dtype)], axis=-2)
 
 
-def layer_norm(values, gain, axis):
+def layer_norm(values, axis):
     middle = jnp.mean(values, axis=axis, keepdims=True)
     centred = values - middle
     spread = jnp.mean(centred * centred, axis=axis, keepdims=True)
-    return centred * lax.rsqrt(spread + EPS) * gain
+    return centred * lax.rsqrt(spread + EPS)
 
 
 def triangle_kernel(
@@ -63,7 +63,7 @@
     lax.fori_loop(1, devices, greet, 0)
 
     for low, high in chunks(cols, 8):
-        normed = layer_norm(pair_ref[:, low:high, :].astype(jnp.float32), in_gain_ref[...], -1)
+        normed = layer_norm(pair_ref[:, low:high, :].astype(jnp.float32), -1) * in_gain_ref[...]
         turned[low:high] = pad_rows(jnp.transpose(normed, (1, 0, 2)), padded).astype(jnp.bfloat16)
 
     def make(side):
@@ -173,7 +173,7 @@
 
         lax.fori_loop(1, fellows, one, 0)
 
-    ahead = min(3, steps - ends)
+    ahead = steps - ends
 
     @pl.when(middle == 1)
     def _():
@@ -222,9 +222,10 @@
             wait_for(everyone, left_sent.at[h])
             wait_for(everyone, right_sent.at[h])
 
+    out_gain = jnp.transpose(jnp.broadcast_to(out_gain_ref[...], (padded, hidden)))
     for low, high in chunks(cols, 8):
         tri = landed[:, :, :, low:high, :].astype(jnp.float32).reshape(hidden, high - low, padded)
-        tri = jnp.transpose(layer_norm(tri, out_gain_ref[...], 0), (1, 0, 2)).astype(jnp.bfloat16)
+        tri = (jnp.transpose(layer_norm(tri, 0), (1, 0, 2)) * out_gain).astype(jnp.bfloat16)
         mixed = []
         for at in range(low, high):
             mix = lax.dot_general(
@@ -241,7 +242,7 @@
     fellows = n_row * (n_col // 2)
     owners = n_row * (n_col // 4)
     part = hidden // owners
-    per = max(part // 8, 1)
+    per = max(part // 16, 1)
     steps = part // per
     ends = steps // 4
     padded = -(-rows // LANES) * LANES
@@ -269,7 +270,7 @@
         ln_in_gain.reshape(1, 1, channels),
         proj_ab,
         gate_weight,
-        ln_out_gain.reshape(hidden, 1, 1),
+        ln_out_gain.reshape(1, hidden),
         out_weight,
     )
 

time: 105 us -> 102 us (0.971)
  Pallas kernels: 101 us -> 99.3 us
  local copies, waits for them, and re-layouts: 4.09 us -> 2.7 us
    pallas_call x1, Pallas kernels: 101 us -> 99.3 us  [shards(): pl.pallas_call(functools.partial(triangle_kernel, n_row, n_col, ends), ou...]
    reshape x1 -> x0, local copies, waits for them, and re-layouts: 1.39 us -> none  [shards(): ln_out_gain.reshape(hidden, 1, 1)]
where the time goes in v6:
time: 102 us
  Pallas kernels  99.3 us (97%)
  local copies, waits for them, and re-layouts  2.7 us (3%)
    pallas_call x1, Pallas kernels, shards(): pl.pallas_call(functools.partial(triangle_kernel, n_row, n_col, ends), ou...  99.3 us
    unnamed x1, local copies, waits for them, and re-layouts  2.7 us

profile of v6, /device:TPU:0, one launch (start us, length us, event | category | flops | bytes accessed | tf_op | source)
XLA Modules:
  0.0 102.0 jit_solution(10198278888433643107)
XLA Ops:
  0.0 99.3 %triangle.1 = bf16[112,56,128]{2,1,0:T(8,128)(2,1)} custom-call(bf16[112,56,128]{2,1,0:T(8,128)(2,1)} %pair_ref.1, s32[56,112]{1,0:T(8,128)} %bitcast.3, f32[1,1,128]{2,1,0:T(1,128)} %bitcast.4, bf16[128,512]{1,0:T(8,128)(2,1)} %proj_ref.1, bf16[128,128]{1,0:T(8,128)(2,1)} %gate_ref.1, f32[1,128]{1,0:T(1,128)} %bitcast.5, bf16[128,128]{1,0:T(8,128)(2,1)} %weight_ref.1), custom_call_target="tpu_custom_call" | custom-call | tf_op jit(solution)/shard_map/triangle/pallas_call | solution.py:250
  99.3 2.7 %copy.9 = bf16[112,56,128]{2,1,0:T(8,128)(2,1)} copy(bf16[112,56,128]{2,1,0:T(8,128)(2,1)} %triangle.1) | data formatting | bytes 3211264

commit v7 on v6

--- a/solution.py
+++ b/solution.py
@@ -122,8 +122,9 @@
     send(0, ends)
     for h in range(ends):
         send_far(h)
+    for h in range(ends + 1, steps):
         send(0, h)
-    for h in range(ends + 1, steps):
+    for h in range(ends):
         send(0, h)
     make(1)
     for h in range(steps):
@@ -232,7 +233,7 @@
                 tri[at - low], weight_ref[...], (((0,), (0,)), ((), ())), preferred_element_type=jnp.float32
             )
             mixed.append((gates[at] * mix)[:rows])
-        update_ref[:, low:high, :] = jnp.transpose(jnp.stack(mixed), (1, 0, 2)).astype(jnp.bfloat16)
+        update_ref[low:high] = jnp.stack(mixed).astype(jnp.bfloat16)
 
 
 def shards(pair, pair_mask, ln_in_gain, proj_ab, gate_weight, ln_out_gain, out_weight):
@@ -249,7 +250,7 @@
     block = (per, cols, padded)
     return pl.pallas_call(
         functools.partial(triangle_kernel, n_row, n_col, ends),
-        out_shape=jax.ShapeDtypeStruct((rows, cols, channels), jnp.bfloat16),
+        out_shape=jax.ShapeDtypeStruct((cols, rows, channels), jnp.bfloat16),
         in_specs=[VMEM] * 7,
         out_specs=VMEM,
         scratch_shapes=[
@@ -272,7 +273,7 @@
         gate_weight,
         ln_out_gain.reshape(1, hidden),
         out_weight,
-    )
+    ).transpose(1, 0, 2)
 
 
 def solution(mesh):

time: 102 us -> 102 us (level)
    transpose x0 -> x1, local copies, waits for them, and re-layouts: none -> 2.99 us  [shards(): return pl.pallas_call(functools.partial(triangle_kernel, n_row, n_col, en...]
    unnamed x1 -> x0, local copies, waits for them, and re-layouts: 2.7 us -> none
where the time goes in v7:
time: 102 us
  Pallas kernels  98.8 us (97%)
  local copies, waits for them, and re-layouts  2.99 us (3%)
    pallas_call x1, Pallas kernels, shards(): pl.pallas_call(functools.partial(triangle_kernel, n_row, n_col, ends), ou...  98.8 us
    transpose x1, local copies, waits for them, and re-layouts, shards(): return pl.pallas_call(functools.partial(triangle_kernel, n_row, n_col, en...  2.99 us

profile of v7, /device:TPU:0, one launch (start us, length us, event | category | flops | bytes accessed | tf_op | source)
XLA Modules:
  0.0 101.8 jit_solution(2866551293720500048)
XLA Ops:
  0.0 98.8 %triangle.1 = bf16[56,112,128]{2,1,0:T(8,128)(2,1)} custom-call(bf16[112,56,128]{2,1,0:T(8,128)(2,1)} %pair_ref.1, s32[56,112]{1,0:T(8,128)} %bitcast.5, f32[1,1,128]{2,1,0:T(1,128)} %bitcast.6, bf16[128,512]{1,0:T(8,128)(2,1)} %proj_ref.1, bf16[128,128]{1,0:T(8,128)(2,1)} %gate_ref.1, f32[1,128]{1,0:T(1,128)} %bitcast.7, bf16[128,128]{1,0:T(8,128)(2,1)} %weight_ref.1), custom_call_target="tpu_custom_call" | custom-call | tf_op jit(solution)/shard_map/triangle/pallas_call | solution.py:251
  98.8 3.0 %copy.8 = bf16[112,56,128]{2,1,0:T(8,128)(2,1)} copy(bf16[112,56,128]{2,0,1:T(8,128)(2,1)} %bitcast.4) | data formatting | bytes 3211264 | tf_op jit(solution)/shard_map/transpose | solution.py:276
